TPU v7x, 512 devices: a whole 4x8x8 slice. The times are simulated.
512 devices in a mesh: heads: 8 (over z_lo, core), tm: 64 (over x, y, z_hi).
Axes of the slice: x: 4, y: 8, z: 8 (z_hi: 2, z_lo: 4; z = z_hi * 4 + z_lo), core: 2. Of those that a mesh axis runs over, the one named last changes fastest.
Arguments:
- queries: bfloat16 [16384, 3072], P('tm', 'heads'), parts along dimension 1, may hold values from -8 to 8
- keys: bfloat16 [16384, 3072], P('tm', 'heads'), parts along dimension 1, may hold values from -8 to 8
- values: bfloat16 [16384, 3072], P('tm', 'heads'), parts along dimension 1, may hold values from -6 to 6
- positions: int32 [3, 16384], P(None, 'tm'), may hold values from 0 to 79, as said below
- tile_masks: int32 [128, 8, 2], P('tm'), may hold values from 0 to 1, as said below
- sink_index: int32 [256], replicated, may hold values from 0 to 3599, as said below
Outputs:
- attended: bfloat16 [16384, 3072], P('tm', 'heads'), parts along dimension 1
There are 8 independent parts, one for each index of `heads`. A program takes and returns all parts, laid end to end along the dimension named above; an argument that names none is the same for every part. Nothing has to cross between parts.
Inputs may be any that keep to these rules, and one draw needn't show every extreme that they name: `positions`: consecutive tokens of the latent video of 33 x 45 x 80, row by row, from some starting token. `tile_masks`: tiles of farther partners are kept less often. `sink_index`: distinct rows among the first min(16384, 3600) of the window.
All inputs are finite; a program needn't handle non-finite values.
Results may differ from a plain program's by a relative error of at most 0.0085.
The roundings to bfloat16 on the way count: a program that leaves them out, or rounds other values in their place, can miss the bound.
Values may be sent and summed in bfloat16 or wider, within the bound.
A program may use at most 64 MiB of HBM per device.

v0:
```python
import jax
import jax.numpy as jnp
from jax import lax
from jax.sharding import PartitionSpec as P

HG = 3
HD = 128
TILE = 128
NOFF = 4
SINK = 256


def shifted(shard, axis, by):
    length = lax.axis_size(axis)
    pairs = [(i, i + by) for i in range(length) if 0 <= i + by < length]
    return lax.ppermute(shard, axis, pairs)


def rotate(row_data, position, factor):
    row_count = row_data.shape[0]
    first_size = HD // 8
    second_size = (HD - HD // 8) // 2
    section_sizes = (first_size, second_size, HD - first_size - second_size)
    angle_list = []
    for axis_id in range(3):
        section_width = section_sizes[axis_id]
        inverse = 256.0 ** (-jnp.arange(0, section_width, 2).astype(jnp.float32) / section_width)
        angle_list.append(position[axis_id].astype(jnp.float32)[:, None] * inverse[None, :])
    angle_all = jnp.concatenate(angle_list, axis=1)
    cosine = jnp.cos(angle_all)[:, None, :]
    sine_part = jnp.sin(angle_all)[:, None, :]
    pair_view = row_data.astype(jnp.float32).reshape(row_count, HG, HD // 2, 2)
    even_part = pair_view[..., 0]
    odd_part = pair_view[..., 1]
    turned = jnp.stack(
        [even_part * cosine - odd_part * sine_part, even_part * sine_part + odd_part * cosine],
        axis=-1,
    )
    return (turned * factor).reshape(row_count, HG * HD)


def block_part(query_heads, key_heads, value_heads, tile_keep):
    keep_mask = jnp.repeat(jnp.repeat(tile_keep, TILE, axis=0), TILE, axis=1)[:, None, :]
    scores = jnp.einsum("qhd,khd->qhk", query_heads, key_heads, preferred_element_type=jnp.float32)
    masked = jnp.where(keep_mask > 0, scores, -1e30)
    row_max = jnp.max(masked, axis=2)
    weights = jnp.exp(masked - row_max[:, :, None]) * keep_mask
    totals = jnp.sum(weights, axis=2)
    weighted = jnp.einsum(
        "qhk,khd->qhd",
        weights.astype(jnp.bfloat16),
        value_heads,
        preferred_element_type=jnp.float32,
    )
    return (weighted, row_max, totals)


def combine_parts(first, second):
    weighted_a, max_a, total_a = first
    weighted_b, max_b, total_b = second
    new_max = jnp.maximum(max_a, max_b)
    scale_first = jnp.exp(max_a - new_max)
    scale_second = jnp.exp(max_b - new_max)
    weighted = weighted_a * scale_first[:, :, None] + weighted_b * scale_second[:, :, None]
    return (weighted, new_max, total_a * scale_first + total_b * scale_second)


def on_device(queries, keys, values, positions, tile_masks, sink_index):
    rows_here = queries.shape[0]
    shards = lax.axis_size("tm")
    index_here = lax.axis_index("tm")
    feature_width = HG * HD
    tiles = rows_here // TILE
    q_rot = rotate(queries, positions, HD ** (-0.5)).astype(jnp.bfloat16)
    k_rot = rotate(keys, positions, 1.0).astype(jnp.bfloat16)
    query_heads = q_rot.reshape(rows_here, HG, HD)
    key_heads = k_rot.reshape(rows_here, HG, HD)
    value_heads = values.reshape(rows_here, HG, HD)
    state = block_part(query_heads, key_heads, value_heads, jnp.ones((tiles, tiles), jnp.float32))
    local_index = sink_index - index_here * rows_here
    one_hot = (local_index[:, None] == jnp.arange(rows_here, dtype=jnp.int32)[None, :]).astype(
        jnp.bfloat16
    )
    sink_table = jnp.dot(
        one_hot, jnp.concatenate([k_rot, values], axis=1), preferred_element_type=jnp.float32
    )
    sink_table = lax.psum(sink_table, "tm").astype(jnp.bfloat16)
    sink_keys = sink_table[:, :feature_width].reshape(SINK, HG, HD)
    sink_values = sink_table[:, feature_width:].reshape(SINK, HG, HD)
    sink_keep = jnp.ones((tiles, SINK // TILE), jnp.float32)
    state = combine_parts(state, block_part(query_heads, sink_keys, sink_values, sink_keep))
    mask_float = tile_masks.astype(jnp.float32)
    for offset in range(1, NOFF + 1):
        reverse_mask = tile_masks[:, NOFF + offset - 1, :].astype(jnp.bfloat16)
        their_queries, their_keys, their_values, their_mask = shifted(
            (q_rot, k_rot, values, reverse_mask), "tm", -offset
        )
        later_ok = (index_here + offset < shards).astype(jnp.float32)
        earlier_ok = (index_here - offset >= 0).astype(jnp.float32)
        mine_part = block_part(
            query_heads,
            their_keys.reshape(rows_here, HG, HD),
            their_values.reshape(rows_here, HG, HD),
            mask_float[:, offset - 1, :] * later_ok,
        )
        state = combine_parts(state, mine_part)
        returned = block_part(
            their_queries.reshape(rows_here, HG, HD),
            key_heads,
            value_heads,
            their_mask.astype(jnp.float32),
        )
        back_weighted, back_max, back_totals = shifted(
            (returned[0], returned[1], returned[2]), "tm", offset
        )
        back_max = jnp.where(earlier_ok > 0, back_max, -1e30)
        state = combine_parts(
            state, (back_weighted * earlier_ok, back_max, back_totals * earlier_ok)
        )
    weighted, row_max, totals = state
    return (weighted / totals[:, :, None]).astype(jnp.bfloat16).reshape(rows_here, feature_width)


def solution(mesh):
    in_specs = (
        P("tm", "heads"),
        P("tm", "heads"),
        P("tm", "heads"),
        P(None, "tm"),
        P("tm", None, None),
        P(),
    )
    out_specs = P("tm", "heads")
    return jax.shard_map(
        on_device, mesh=mesh, in_specs=in_specs, out_specs=out_specs, check_vma=False
    )
```

profile of v0, /device:TPU:4, one launch (start us, length us, event | category | flops | bytes accessed | tf_op | source)
XLA Modules:
  0.0 699.2 jit_solution(151011124536786140)
XLA Ops:
  0.0 13.8 %collective-permute-start.1 = (bf16[256,384]{1,0:T(8,128)(2,1)}, bf16[256,384]{1,0:T(8,128)(2,1)}, u32[]{:S(2)}, u32[]{:S(2)}) collective-permute-start(bf16[256,384]{1,0:T(8,128)(2,1)} %param.8), channel_id=1, source_target_pairs={{1,0},{2,1},{3,2},{4,3},{5,4},{6,5},{7,6},{8,7},{9,8},{10,9},{11,1... | collective-permute-start | bytes 589832 | tf_op jit(solution)/shard_map/ppermute | solution.py:16
  33.5 404.2 %all-reduce.1 = bf16[256,768]{1,0:T(8,128)(2,1)S(1)} all-reduce(f32[256,768]{1,0:T(8,128)S(1)} %fusion.64), channel_id=1, replica_groups=mesh['heads'=8,'tm'=64] {'tm'}, use_global_device_ids=true, to_apply=%region_1.2 | all-reduce | flops 196608 | bytes 1179648 | tf_op jit(solution)/shard_map/psum | solution.py:87
  442.4 8.1 %collective-permute-done.14 = bf16[2,2]{1,0:T(2,128)(2,1)S(1)} collective-permute-done((bf16[2,2]{1,0:T(2,128)(2,1)S(1)}, bf16[2,2]{1,0:T(2,128)(2,1)S(1)}, u32[]{:S(2)}, u32[]{:S(2)}) %collective-permute-start.14) | collective-permute-done | bytes 40 | tf_op jit(solution)/shard_map/ppermute | solution.py:16
  450.6 7.0 %collective-permute-start.8 = (bf16[2,2]{1,0:T(2,128)(2,1)S(1)}, bf16[2,2]{1,0:T(2,128)(2,1)S(1)}, u32[]{:S(2)}, u32[]{:S(2)}) collective-permute-start(bf16[2,2]{1,0:T(2,128)(2,1)S(1)} %get-tuple-element.7), channel_id=1, source_target_pairs={{2,0},{3,1},{4,2},{5,3},{6,4},{7,5},{8,6},{9,7},{10,8},{11,9},{12,... | collective-permute-start | bytes 32 | tf_op jit(solution)/shard_map/ppermute | solution.py:16
  463.0 5.3 collective-permute-done.2
  468.2 6.7 collective-permute-start.15
  475.2 6.5 collective-permute-done.15
  481.6 11.3 %collective-permute-start = (bf16[256,384]{0,1:T(8,128)(2,1)S(1)}, bf16[256,384]{0,1:T(8,128)(2,1)S(1)}, u32[]{:S(2)}, u32[]{:S(2)}) collective-permute-start(bf16[256,384]{0,1:T(8,128)(2,1)S(1)} %convert_element_type.180), channel_id=1, source_target_pairs={{1,0},{2,1},{3,2},{4,3},{5,4},{6,5},{7,6},{8,7},{9,8},{10,9},{11,1... | collective-permute-start | bytes 589832 | tf_op jit(solution)/shard_map/ppermute | solution.py:16
  496.1 11.2 %collective-permute-start.6 = (bf16[256,384]{0,1:T(8,128)(2,1)S(1)}, bf16[256,384]{0,1:T(8,128)(2,1)S(1)}, u32[]{:S(2)}, u32[]{:S(2)}) collective-permute-start(bf16[256,384]{0,1:T(8,128)(2,1)S(1)} %convert_element_type.180), channel_id=1, source_target_pairs={{2,0},{3,1},{4,2},{5,3},{6,4},{7,5},{8,6},{9,7},{10,8},{11,9},{12,... | collective-permute-start | bytes 589832 | tf_op jit(solution)/shard_map/ppermute | solution.py:16
  514.7 8.0 %collective-permute-done.12 = bf16[256,384]{0,1:T(8,128)(2,1)S(1)} collective-permute-done((bf16[256,384]{0,1:T(8,128)(2,1)S(1)}, bf16[256,384]{0,1:T(8,128)(2,1)S(1)}, u32[]{:S(2)}, u32[]{:S(2)}) %collective-permute-start.12) | collective-permute-done | bytes 196640 | tf_op jit(solution)/shard_map/ppermute | solution.py:16
  527.0 7.3 %collective-permute-done.18 = bf16[256,384]{0,1:T(8,128)(2,1)S(1)} collective-permute-done((bf16[256,384]{0,1:T(8,128)(2,1)S(1)}, bf16[256,384]{0,1:T(8,128)(2,1)S(1)}, u32[]{:S(2)}, u32[]{:S(2)}) %collective-permute-start.18) | collective-permute-done | bytes 196640 | tf_op jit(solution)/shard_map/ppermute | solution.py:16
  537.6 5.2 collective-permute-done.21
  542.8 9.7 %collective-permute-start.9 = (bf16[256,384]{0,1:T(8,128)(2,1)S(1)}, bf16[256,384]{0,1:T(8,128)(2,1)S(1)}, u32[]{:S(2)}, u32[]{:S(2)}) collective-permute-start(bf16[256,384]{0,1:T(8,128)(2,1)S(1)} %convert_element_type.189), channel_id=1, source_target_pairs={{2,0},{3,1},{4,2},{5,3},{6,4},{7,5},{8,6},{9,7},{10,8},{11,9},{12,... | collective-permute-start | bytes 589832 | tf_op jit(solution)/shard_map/ppermute | solution.py:16
  557.8 7.4 %collective-permute-start.3 = (bf16[256,384]{0,1:T(8,128)(2,1)S(1)}, bf16[256,384]{0,1:T(8,128)(2,1)S(1)}, u32[]{:S(2)}, u32[]{:S(2)}) collective-permute-start(bf16[256,384]{0,1:T(8,128)(2,1)S(1)} %convert_element_type.189), channel_id=1, source_target_pairs={{1,0},{2,1},{3,2},{4,3},{5,4},{6,5},{7,6},{8,7},{9,8},{10,9},{11,1... | collective-permute-start | bytes 589832 | tf_op jit(solution)/shard_map/ppermute | solution.py:16
  569.3 15.0 %collective-permute-start.16 = (f32[256,3]{0,1:T(4,128)S(1)}, f32[256,3]{0,1:T(4,128)S(1)}, u32[]{:S(2)}, u32[]{:S(2)}) collective-permute-start(f32[256,3]{0,1:T(4,128)S(1)} %get-tuple-element.55), channel_id=1, source_target_pairs={{0,3},{1,4},{2,5},{3,6},{4,7},{5,8},{6,9},{7,10},{8,11},{9,12},{10... | collective-permute-start | bytes 9224 | tf_op jit(solution)/shard_map/ppermute | solution.py:16
  589.2 9.7 %collective-permute-start.10 = (f32[256,3]{0,1:T(4,128)S(1)}, f32[256,3]{0,1:T(4,128)S(1)}, u32[]{:S(2)}, u32[]{:S(2)}) collective-permute-start(f32[256,3]{0,1:T(4,128)S(1)} %get-tuple-element.59), channel_id=1, source_target_pairs={{0,2},{1,3},{2,4},{3,5},{4,6},{5,7},{6,8},{7,9},{8,10},{9,11},{10,... | collective-permute-start | bytes 9224 | tf_op jit(solution)/shard_map/ppermute | solution.py:16
  604.5 9.0 %collective-permute-start.22 = (f32[256,3]{0,1:T(4,128)S(1)}, f32[256,3]{0,1:T(4,128)S(1)}, u32[]{:S(2)}, u32[]{:S(2)}) collective-permute-start(f32[256,3]{0,1:T(4,128)S(1)} %get-tuple-element.53), channel_id=1, source_target_pairs={{0,4},{1,5},{2,6},{3,7},{4,8},{5,9},{6,10},{7,11},{8,12},{9,13},{1... | collective-permute-start | bytes 9224 | tf_op jit(solution)/shard_map/ppermute | solution.py:16
  615.2 15.9 %collective-permute-start.27 = (f32[256,3]{0,1:T(4,128)S(1)}, f32[256,3]{0,1:T(4,128)S(1)}, u32[]{:S(2)}, u32[]{:S(2)}) collective-permute-start(f32[256,3]{0,1:T(4,128)S(1)} %fusion.51), channel_id=1, source_target_pairs={{0,4},{1,5},{2,6},{3,7},{4,8},{5,9},{6,10},{7,11},{8,12},{9,13},{1... | collective-permute-start | bytes 9224 | tf_op jit(solution)/shard_map/ppermute | solution.py:16
  632.9 8.1 %collective-permute-start.26 = (f32[256,3]{0,1:T(4,128)S(1)}, f32[256,3]{0,1:T(4,128)S(1)}, u32[]{:S(2)}, u32[]{:S(2)}) collective-permute-start(f32[256,3]{0,1:T(4,128)S(1)} %fusion.47), channel_id=1, source_target_pairs={{0,3},{1,4},{2,5},{3,6},{4,7},{5,8},{6,9},{7,10},{8,11},{9,12},{10... | collective-permute-start | bytes 9224 | tf_op jit(solution)/shard_map/ppermute | solution.py:16
  644.5 7.3 %collective-permute-start.24 = (f32[256,3]{0,1:T(4,128)S(1)}, f32[256,3]{0,1:T(4,128)S(1)}, u32[]{:S(2)}, u32[]{:S(2)}) collective-permute-start(f32[256,3]{0,1:T(4,128)S(1)} %fusion.39), channel_id=1, source_target_pairs={{0,1},{1,2},{2,3},{3,4},{4,5},{5,6},{6,7},{7,8},{8,9},{9,10},{10,1... | collective-permute-start | bytes 9224 | tf_op jit(solution)/shard_map/ppermute | solution.py:16
  651.8 11.9 %collective-permute-start.23 = (f32[256,3,128]{0,2,1:T(8,128)}, f32[256,3,128]{0,2,1:T(8,128)S(1)}, u32[]{:S(2)}, u32[]{:S(2)}) collective-permute-start(f32[256,3,128]{0,2,1:T(8,128)} %convolution_bitcast_fusion.10), channel_id=1, source_target_pairs={{0,4},{1,5},{2,6},{3,7},{4,8},{5,9},{6,10},{7,11},{8,12},{9,13},{1... | collective-permute-start | bytes 1179656 | tf_op jit(solution)/shard_map/ppermute | solution.py:16
  668.2 7.3 %collective-permute-start.5 = (f32[256,3,128]{0,2,1:T(8,128)}, f32[256,3,128]{0,2,1:T(8,128)S(1)}, u32[]{:S(2)}, u32[]{:S(2)}) collective-permute-start(f32[256,3,128]{0,2,1:T(8,128)} %convolution_bitcast_fusion.16), channel_id=1, source_target_pairs={{0,1},{1,2},{2,3},{3,4},{4,5},{5,6},{6,7},{7,8},{8,9},{9,10},{10,1... | collective-permute-start | bytes 1179656 | tf_op jit(solution)/shard_map/ppermute | solution.py:16
  679.8 7.0 %collective-permute-done.17 = f32[256,3,128]{0,2,1:T(8,128)S(1)} collective-permute-done((f32[256,3,128]{0,2,1:T(8,128)}, f32[256,3,128]{0,2,1:T(8,128)S(1)}, u32[]{:S(2)}, u32[]{:S(2)}) %collective-permute-start.17) | collective-permute-done | bytes 393248 | tf_op jit(solution)/shard_map/ppermute | solution.py:16
  686.8 11.1 %collective-permute-done.5 = f32[256,3,128]{0,2,1:T(8,128)S(1)} collective-permute-done((f32[256,3,128]{0,2,1:T(8,128)}, f32[256,3,128]{0,2,1:T(8,128)S(1)}, u32[]{:S(2)}, u32[]{:S(2)}) %collective-permute-start.5) | collective-permute-done | bytes 393248 | tf_op jit(solution)/shard_map/ppermute | solution.py:16
  (164 shorter events, 84.4 us)
Async XLA Ops:
  0.0 589.1 %collective-permute-start.1 = (bf16[256,384]{1,0:T(8,128)(2,1)}, bf16[256,384]{1,0:T(8,128)(2,1)}, u32[]{:S(2)}, u32[]{:S(2)}) collective-permute-start(bf16[256,384]{1,0:T(8,128)(2,1)} %param.8), channel_id=1, source_target_pairs={{1,0},{2,1},{3,2},{4,3},{5,4},{6,5},{7,6},{8,7},{9,8},{10,9},{11,1... | collective-permute-start | bytes 589832 | tf_op jit(solution)/shard_map/ppermute | solution.py:16
  13.8 585.1 %collective-permute-start.7 = (bf16[256,384]{1,0:T(8,128)(2,1)}, bf16[256,384]{1,0:T(8,128)(2,1)}, u32[]{:S(2)}, u32[]{:S(2)}) collective-permute-start(bf16[256,384]{1,0:T(8,128)(2,1)} %param.8), channel_id=1, source_target_pairs={{2,0},{3,1},{4,2},{5,3},{6,4},{7,5},{8,6},{9,7},{10,8},{11,9},{12,... | collective-permute-start | bytes 589832 | tf_op jit(solution)/shard_map/ppermute | solution.py:16
  17.1 587.4 %collective-permute-start.19 = (bf16[256,384]{1,0:T(8,128)(2,1)}, bf16[256,384]{1,0:T(8,128)(2,1)}, u32[]{:S(2)}, u32[]{:S(2)}) collective-permute-start(bf16[256,384]{1,0:T(8,128)(2,1)} %param.8), channel_id=1, source_target_pairs={{4,0},{5,1},{6,2},{7,3},{8,4},{9,5},{10,6},{11,7},{12,8},{13,9},{1... | collective-permute-start | bytes 589832 | tf_op jit(solution)/shard_map/ppermute | solution.py:16
  21.1 594.1 %collective-permute-start.13 = (bf16[256,384]{1,0:T(8,128)(2,1)}, bf16[256,384]{1,0:T(8,128)(2,1)}, u32[]{:S(2)}, u32[]{:S(2)}) collective-permute-start(bf16[256,384]{1,0:T(8,128)(2,1)} %param.8), channel_id=1, source_target_pairs={{3,0},{4,1},{5,2},{6,3},{7,4},{8,5},{9,6},{10,7},{11,8},{12,9},{13... | collective-permute-start | bytes 589832 | tf_op jit(solution)/shard_map/ppermute | solution.py:16
  24.0 416.4 %collective-permute-start.20 = (bf16[2,2]{1,0:T(2,128)(2,1)S(1)}, bf16[2,2]{1,0:T(2,128)(2,1)S(1)}, u32[]{:S(2)}, u32[]{:S(2)}) collective-permute-start(bf16[2,2]{1,0:T(2,128)(2,1)S(1)} %get-tuple-element.5), channel_id=1, source_target_pairs={{4,0},{5,1},{6,2},{7,3},{8,4},{9,5},{10,6},{11,7},{12,8},{13,9},{1... | collective-permute-start | bytes 32 | tf_op jit(solution)/shard_map/ppermute | solution.py:16
  468.2 13.4 %collective-permute-start.15 = (bf16[256,384]{0,1:T(8,128)(2,1)S(1)}, bf16[256,384]{0,1:T(8,128)(2,1)S(1)}, u32[]{:S(2)}, u32[]{:S(2)}) collective-permute-start(bf16[256,384]{0,1:T(8,128)(2,1)S(1)} %convert_element_type.189), channel_id=1, source_target_pairs={{3,0},{4,1},{5,2},{6,3},{7,4},{8,5},{9,6},{10,7},{11,8},{12,9},{13... | collective-permute-start | bytes 589832 | tf_op jit(solution)/shard_map/ppermute | solution.py:16
  481.6 14.4 %collective-permute-start = (bf16[256,384]{0,1:T(8,128)(2,1)S(1)}, bf16[256,384]{0,1:T(8,128)(2,1)S(1)}, u32[]{:S(2)}, u32[]{:S(2)}) collective-permute-start(bf16[256,384]{0,1:T(8,128)(2,1)S(1)} %convert_element_type.180), channel_id=1, source_target_pairs={{1,0},{2,1},{3,2},{4,3},{5,4},{6,5},{7,6},{8,7},{9,8},{10,9},{11,1... | collective-permute-start | bytes 589832 | tf_op jit(solution)/shard_map/ppermute | solution.py:16
  496.1 14.3 %collective-permute-start.6 = (bf16[256,384]{0,1:T(8,128)(2,1)S(1)}, bf16[256,384]{0,1:T(8,128)(2,1)S(1)}, u32[]{:S(2)}, u32[]{:S(2)}) collective-permute-start(bf16[256,384]{0,1:T(8,128)(2,1)S(1)} %convert_element_type.180), channel_id=1, source_target_pairs={{2,0},{3,1},{4,2},{5,3},{6,4},{7,5},{8,6},{9,7},{10,8},{11,9},{12,... | collective-permute-start | bytes 589832 | tf_op jit(solution)/shard_map/ppermute | solution.py:16
  510.4 12.4 %collective-permute-start.12 = (bf16[256,384]{0,1:T(8,128)(2,1)S(1)}, bf16[256,384]{0,1:T(8,128)(2,1)S(1)}, u32[]{:S(2)}, u32[]{:S(2)}) collective-permute-start(bf16[256,384]{0,1:T(8,128)(2,1)S(1)} %convert_element_type.180), channel_id=1, source_target_pairs={{3,0},{4,1},{5,2},{6,3},{7,4},{8,5},{9,6},{10,7},{11,8},{12,9},{13... | collective-permute-start | bytes 589832 | tf_op jit(solution)/shard_map/ppermute | solution.py:16
  522.8 11.5 %collective-permute-start.18 = (bf16[256,384]{0,1:T(8,128)(2,1)S(1)}, bf16[256,384]{0,1:T(8,128)(2,1)S(1)}, u32[]{:S(2)}, u32[]{:S(2)}) collective-permute-start(bf16[256,384]{0,1:T(8,128)(2,1)S(1)} %convert_element_type.180), channel_id=1, source_target_pairs={{4,0},{5,1},{6,2},{7,3},{8,4},{9,5},{10,6},{11,7},{12,8},{13,9},{1... | collective-permute-start | bytes 589832 | tf_op jit(solution)/shard_map/ppermute | solution.py:16
  542.8 15.0 %collective-permute-start.9 = (bf16[256,384]{0,1:T(8,128)(2,1)S(1)}, bf16[256,384]{0,1:T(8,128)(2,1)S(1)}, u32[]{:S(2)}, u32[]{:S(2)}) collective-permute-start(bf16[256,384]{0,1:T(8,128)(2,1)S(1)} %convert_element_type.189), channel_id=1, source_target_pairs={{2,0},{3,1},{4,2},{5,3},{6,4},{7,5},{8,6},{9,7},{10,8},{11,9},{12,... | collective-permute-start | bytes 589832 | tf_op jit(solution)/shard_map/ppermute | solution.py:16
  557.8 11.5 %collective-permute-start.3 = (bf16[256,384]{0,1:T(8,128)(2,1)S(1)}, bf16[256,384]{0,1:T(8,128)(2,1)S(1)}, u32[]{:S(2)}, u32[]{:S(2)}) collective-permute-start(bf16[256,384]{0,1:T(8,128)(2,1)S(1)} %convert_element_type.189), channel_id=1, source_target_pairs={{1,0},{2,1},{3,2},{4,3},{5,4},{6,5},{7,6},{8,7},{9,8},{10,9},{11,1... | collective-permute-start | bytes 589832 | tf_op jit(solution)/shard_map/ppermute | solution.py:16
  569.3 63.5 %collective-permute-start.16 = (f32[256,3]{0,1:T(4,128)S(1)}, f32[256,3]{0,1:T(4,128)S(1)}, u32[]{:S(2)}, u32[]{:S(2)}) collective-permute-start(f32[256,3]{0,1:T(4,128)S(1)} %get-tuple-element.55), channel_id=1, source_target_pairs={{0,3},{1,4},{2,5},{3,6},{4,7},{5,8},{6,9},{7,10},{8,11},{9,12},{10... | collective-permute-start | bytes 9224 | tf_op jit(solution)/shard_map/ppermute | solution.py:16
  589.2 51.8 %collective-permute-start.10 = (f32[256,3]{0,1:T(4,128)S(1)}, f32[256,3]{0,1:T(4,128)S(1)}, u32[]{:S(2)}, u32[]{:S(2)}) collective-permute-start(f32[256,3]{0,1:T(4,128)S(1)} %get-tuple-element.59), channel_id=1, source_target_pairs={{0,2},{1,3},{2,4},{3,5},{4,6},{5,7},{6,8},{7,9},{8,10},{9,11},{10,... | collective-permute-start | bytes 9224 | tf_op jit(solution)/shard_map/ppermute | solution.py:16
  598.9 45.6 %collective-permute-start.4 = (f32[256,3]{0,1:T(4,128)S(1)}, f32[256,3]{0,1:T(4,128)S(1)}, u32[]{:S(2)}, u32[]{:S(2)}) collective-permute-start(f32[256,3]{0,1:T(4,128)S(1)} %get-tuple-element.63), channel_id=1, source_target_pairs={{0,1},{1,2},{2,3},{3,4},{4,5},{5,6},{6,7},{7,8},{8,9},{9,10},{10,1... | collective-permute-start | bytes 9224 | tf_op jit(solution)/shard_map/ppermute | solution.py:16
  604.5 59.3 %collective-permute-start.22 = (f32[256,3]{0,1:T(4,128)S(1)}, f32[256,3]{0,1:T(4,128)S(1)}, u32[]{:S(2)}, u32[]{:S(2)}) collective-permute-start(f32[256,3]{0,1:T(4,128)S(1)} %get-tuple-element.53), channel_id=1, source_target_pairs={{0,4},{1,5},{2,6},{3,7},{4,8},{5,9},{6,10},{7,11},{8,12},{9,13},{1... | collective-permute-start | bytes 9224 | tf_op jit(solution)/shard_map/ppermute | solution.py:16
  615.2 36.7 %collective-permute-start.27 = (f32[256,3]{0,1:T(4,128)S(1)}, f32[256,3]{0,1:T(4,128)S(1)}, u32[]{:S(2)}, u32[]{:S(2)}) collective-permute-start(f32[256,3]{0,1:T(4,128)S(1)} %fusion.51), channel_id=1, source_target_pairs={{0,4},{1,5},{2,6},{3,7},{4,8},{5,9},{6,10},{7,11},{8,12},{9,13},{1... | collective-permute-start | bytes 9224 | tf_op jit(solution)/shard_map/ppermute | solution.py:16
  632.9 32.9 %collective-permute-start.26 = (f32[256,3]{0,1:T(4,128)S(1)}, f32[256,3]{0,1:T(4,128)S(1)}, u32[]{:S(2)}, u32[]{:S(2)}) collective-permute-start(f32[256,3]{0,1:T(4,128)S(1)} %fusion.47), channel_id=1, source_target_pairs={{0,3},{1,4},{2,5},{3,6},{4,7},{5,8},{6,9},{7,10},{8,11},{9,12},{10... | collective-permute-start | bytes 9224 | tf_op jit(solution)/shard_map/ppermute | solution.py:16
  641.0 27.2 %collective-permute-start.25 = (f32[256,3]{0,1:T(4,128)S(1)}, f32[256,3]{0,1:T(4,128)S(1)}, u32[]{:S(2)}, u32[]{:S(2)}) collective-permute-start(f32[256,3]{0,1:T(4,128)S(1)} %fusion.43), channel_id=1, source_target_pairs={{0,2},{1,3},{2,4},{3,5},{4,6},{5,7},{6,8},{7,9},{8,10},{9,11},{10,... | collective-permute-start | bytes 9224 | tf_op jit(solution)/shard_map/ppermute | solution.py:16
  644.5 31.0 %collective-permute-start.24 = (f32[256,3]{0,1:T(4,128)S(1)}, f32[256,3]{0,1:T(4,128)S(1)}, u32[]{:S(2)}, u32[]{:S(2)}) collective-permute-start(f32[256,3]{0,1:T(4,128)S(1)} %fusion.39), channel_id=1, source_target_pairs={{0,1},{1,2},{2,3},{3,4},{4,5},{5,6},{6,7},{7,8},{8,9},{9,10},{10,1... | collective-permute-start | bytes 9224 | tf_op jit(solution)/shard_map/ppermute | solution.py:16
  651.8 27.9 %collective-permute-start.23 = (f32[256,3,128]{0,2,1:T(8,128)}, f32[256,3,128]{0,2,1:T(8,128)S(1)}, u32[]{:S(2)}, u32[]{:S(2)}) collective-permute-start(f32[256,3,128]{0,2,1:T(8,128)} %convolution_bitcast_fusion.10), channel_id=1, source_target_pairs={{0,4},{1,5},{2,6},{3,7},{4,8},{5,9},{6,10},{7,11},{8,12},{9,13},{1... | collective-permute-start | bytes 1179656 | tf_op jit(solution)/shard_map/ppermute | solution.py:16
  663.8 23.0 %collective-permute-start.17 = (f32[256,3,128]{0,2,1:T(8,128)}, f32[256,3,128]{0,2,1:T(8,128)S(1)}, u32[]{:S(2)}, u32[]{:S(2)}) collective-permute-start(f32[256,3,128]{0,2,1:T(8,128)} %convolution_bitcast_fusion.12), channel_id=1, source_target_pairs={{0,3},{1,4},{2,5},{3,6},{4,7},{5,8},{6,9},{7,10},{8,11},{9,12},{10... | collective-permute-start | bytes 1179656 | tf_op jit(solution)/shard_map/ppermute | solution.py:16
  665.7 21.1 %collective-permute-start.11 = (f32[256,3,128]{0,2,1:T(8,128)}, f32[256,3,128]{0,2,1:T(8,128)S(1)}, u32[]{:S(2)}, u32[]{:S(2)}) collective-permute-start(f32[256,3,128]{0,2,1:T(8,128)} %convolution_bitcast_fusion.14), channel_id=1, source_target_pairs={{0,2},{1,3},{2,4},{3,5},{4,6},{5,7},{6,8},{7,9},{8,10},{9,11},{10,... | collective-permute-start | bytes 1179656 | tf_op jit(solution)/shard_map/ppermute | solution.py:16
  668.2 29.7 %collective-permute-start.5 = (f32[256,3,128]{0,2,1:T(8,128)}, f32[256,3,128]{0,2,1:T(8,128)S(1)}, u32[]{:S(2)}, u32[]{:S(2)}) collective-permute-start(f32[256,3,128]{0,2,1:T(8,128)} %convolution_bitcast_fusion.16), channel_id=1, source_target_pairs={{0,1},{1,2},{2,3},{3,4},{4,5},{5,6},{6,7},{7,8},{8,9},{9,10},{10,1... | collective-permute-start | bytes 1179656 | tf_op jit(solution)/shard_map/ppermute | solution.py:16
  (19 other events, 257.0 us)
where the time goes:
time: 700 us; the launch traced here: 699 us
  blocking collectives  404 us (58%)
  starting transfers between devices  189 us (27%)
  waiting for transfers between devices  72.8 us (10%)
  local copies, waits for them, and re-layouts  16.8 us (2%)
  matrix products  10.8 us (2%)
    psum x1, blocking collectives, on_device(): sink_table = lax.psum(sink_table, 'tm').astype(jnp.bfloat16)  404 us
    ppermute x28, starting transfers between devices, shifted(): return lax.ppermute(shard, axis, pairs)  189 us
    ppermute x28, waiting for transfers between devices, shifted(): return lax.ppermute(shard, axis, pairs)  72.8 us
  transfers between devices with their start and end apart: 28, of which 13 were waited for; matrix products, arithmetic and copies ran while one was open for 4% of the time, Pallas kernels for 0%

commit v1 on v0

--- a/solution.py
+++ b/solution.py
@@ -8,6 +8,12 @@
 TILE = 128
 NOFF = 4
 SINK = 256
+
+
+def summed_here(array, name):
+    parts = lax.all_gather(array, name, axis=0, tiled=False)
+    summed = parts.sum(axis=0)
+    return summed
 
 
 def shifted(shard, axis, by):
@@ -84,7 +90,7 @@
     sink_table = jnp.dot(
         one_hot, jnp.concatenate([k_rot, values], axis=1), preferred_element_type=jnp.float32
     )
-    sink_table = lax.psum(sink_table, "tm").astype(jnp.bfloat16)
+    sink_table = summed_here(sink_table, "tm").astype(jnp.bfloat16)
     sink_keys = sink_table[:, :feature_width].reshape(SINK, HG, HD)
     sink_values = sink_table[:, feature_width:].reshape(SINK, HG, HD)
     sink_keep = jnp.ones((tiles, SINK // TILE), jnp.float32)

time: 700 us -> 880 us (1.26)
  the two profiles are of different devices: /device:TPU:4 before, /device:TPU:266 now
where the time goes in v1:
time: 880 us; the launch traced here: 878 us
  waiting for transfers between devices  627 us (71%)
  starting transfers between devices  153 us (17%)
  other arithmetic  34.8 us (4%)
  matrix products  29.5 us (3%)
  local copies, waits for them, and re-layouts  20 us (2%)
  between operations  14.2 us (2%)
    all_gather x1, waiting for transfers between devices, summed_here(): parts = lax.all_gather(array, name, axis=0, tiled=False)  586 us
    ppermute x28, starting transfers between devices, shifted(): return lax.ppermute(shard, axis, pairs)  153 us
    ppermute x28, waiting for transfers between devices, shifted(): return lax.ppermute(shard, axis, pairs)  40.5 us
    reduce_sum x1, other arithmetic, summed_here(): summed = parts.sum(axis=0)  18.3 us
  transfers between devices with their start and end apart: 29, of which 9 were waited for; matrix products, arithmetic and copies ran while one was open for 8% of the time, Pallas kernels for 0%

profile of v1, /device:TPU:266, one launch (start us, length us, event | category | flops | bytes accessed | tf_op | source)
XLA Modules:
  0.0 878.5 jit_solution(8296033587206363455)
XLA Ops:
  17.4 11.5 %collective-permute-start = (bf16[256,384]{0,1:T(8,128)(2,1)S(1)}, bf16[256,384]{0,1:T(8,128)(2,1)}, u32[]{:S(2)}, u32[]{:S(2)}) collective-permute-start(bf16[256,384]{0,1:T(8,128)(2,1)S(1)} %convert_element_type.180), channel_id=1, source_target_pairs={{1,0},{2,1},{3,2},{4,3},{5,4},{6,5},{7,6},{8,7},{9,8},{10,9},{11,1... | collective-permute-start | bytes 589832 | tf_op jit(solution)/shard_map/ppermute | solution.py:22
  42.6 11.3 %collective-permute-start.14 = (bf16[2,2]{1,0:T(2,128)(2,1)S(1)}, bf16[2,2]{1,0:T(2,128)(2,1)S(1)}, u32[]{:S(2)}, u32[]{:S(2)}) collective-permute-start(bf16[2,2]{1,0:T(2,128)(2,1)S(1)} %get-tuple-element.6), channel_id=1, source_target_pairs={{3,0},{4,1},{5,2},{6,3},{7,4},{8,5},{9,6},{10,7},{11,8},{12,9},{13... | collective-permute-start | bytes 32 | tf_op jit(solution)/shard_map/ppermute | solution.py:22
  55.2 7.0 collective-permute-start.2
  65.4 10.2 %collective-permute-start.20 = (bf16[2,2]{1,0:T(2,128)(2,1)S(1)}, bf16[2,2]{1,0:T(2,128)(2,1)S(1)}, u32[]{:S(2)}, u32[]{:S(2)}) collective-permute-start(bf16[2,2]{1,0:T(2,128)(2,1)S(1)} %get-tuple-element.5), channel_id=1, source_target_pairs={{4,0},{5,1},{6,2},{7,3},{8,4},{9,5},{10,6},{11,7},{12,8},{13,9},{1... | collective-permute-start | bytes 32 | tf_op jit(solution)/shard_map/ppermute | solution.py:22
  80.4 11.1 %collective-permute-start.3 = (bf16[256,384]{0,1:T(8,128)(2,1)}, bf16[256,384]{0,1:T(8,128)(2,1)S(1)}, u32[]{:S(2)}, u32[]{:S(2)}) collective-permute-start(bf16[256,384]{0,1:T(8,128)(2,1)} %convert_element_type.189), channel_id=1, source_target_pairs={{1,0},{2,1},{3,2},{4,3},{5,4},{6,5},{7,6},{8,7},{9,8},{10,9},{11,1... | collective-permute-start | bytes 589832 | tf_op jit(solution)/shard_map/ppermute | solution.py:22
  98.8 4.9 collective-permute-start.13
  105.6 3.4 collective-permute-done.3
  109.0 6.7 collective-permute-start.19
  118.0 6.8 collective-permute-start.1
  130.3 6.4 collective-permute-start.18
  142.1 7.1 collective-permute-start.16
  150.1 3.9 collective-permute-start.4
  157.7 4.1 collective-permute-start.22
  164.2 6.8 collective-permute-start.24
  183.5 586.3 %all-gather.3.cloned.1.call-done = f32[16384,768]{1,0:T(8,128)} async-done(((f32[256,768]{1,0:T(8,128)}), f32[16384,768]{1,0:T(8,128)}) %all-gather.3.cloned.1.call-update) | async-done | bytes 50331664 | tf_op jit(solution)/shard_map/all_gather | solution.py:14
  769.8 18.3 %reduce_sum.99 = bf16[256,768]{1,0:T(8,128)(2,1)} reduce(f32[64,256,768]{2,1,0:T(8,128)} %bitcast.244, f32[]{:T(128)} %constant.13.clone.1), dimensions={0}, to_apply=%region_1.2 | reduce | flops 12386304 | bytes 50724868 | tf_op jit(solution)/shard_map/reduce_sum | solution.py:15
  793.0 3.4 collective-permute-start.25
  796.4 9.1 %collective-permute-start.26 = (f32[256,3]{0,1:T(4,128)}, f32[256,3]{0,1:T(4,128)}, u32[]{:S(2)}, u32[]{:S(2)}) collective-permute-start(f32[256,3]{0,1:T(4,128)} %fusion.47), channel_id=1, source_target_pairs={{0,3},{1,4},{2,5},{3,6},{4,7},{5,8},{6,9},{7,10},{8,11},{9,12},{10... | collective-permute-start | bytes 9224 | tf_op jit(solution)/shard_map/ppermute | solution.py:22
  805.4 3.5 collective-permute-start.27
  814.7 5.0 collective-permute-start.17
  819.7 6.5 collective-permute-start.5
  826.3 5.5 collective-permute-start.23
  841.4 11.6 %collective-permute-done.5 = f32[256,3,128]{0,2,1:T(8,128)S(1)} collective-permute-done((f32[256,3,128]{0,2,1:T(8,128)}, f32[256,3,128]{0,2,1:T(8,128)S(1)}, u32[]{:S(2)}, u32[]{:S(2)}) %collective-permute-start.5) | collective-permute-done | bytes 393248 | tf_op jit(solution)/shard_map/ppermute | solution.py:22
  853.1 15.9 %collective-permute-done.23 = f32[256,3,128]{0,2,1:T(8,128)S(1)} collective-permute-done((f32[256,3,128]{0,2,1:T(8,128)}, f32[256,3,128]{0,2,1:T(8,128)S(1)}, u32[]{:S(2)}, u32[]{:S(2)}) %collective-permute-start.23) | collective-permute-done | bytes 393248 | tf_op jit(solution)/shard_map/ppermute | solution.py:22
  (173 shorter events, 97.7 us)
Async XLA Ops:
  6.5 763.3 %all-gather.3.cloned.1.call-start = ((), (), s32[]{:S(2)}) async-start(), calls=%async_computation | async-start | bytes 51118080 | tf_op jit(solution)/shard_map/all_gather | solution.py:14
  13.1 67.2 %collective-permute-start.12 = (bf16[256,384]{0,1:T(8,128)(2,1)S(1)}, bf16[256,384]{0,1:T(8,128)(2,1)S(1)}, u32[]{:S(2)}, u32[]{:S(2)}) collective-permute-start(bf16[256,384]{0,1:T(8,128)(2,1)S(1)} %convert_element_type.180), channel_id=1, source_target_pairs={{3,0},{4,1},{5,2},{6,3},{7,4},{8,5},{9,6},{10,7},{11,8},{12,9},{13... | collective-permute-start | bytes 589832 | tf_op jit(solution)/shard_map/ppermute | solution.py:22
  15.1 76.8 %collective-permute-start.6 = (bf16[256,384]{0,1:T(8,128)(2,1)S(1)}, bf16[256,384]{0,1:T(8,128)(2,1)S(1)}, u32[]{:S(2)}, u32[]{:S(2)}) collective-permute-start(bf16[256,384]{0,1:T(8,128)(2,1)S(1)} %convert_element_type.180), channel_id=1, source_target_pairs={{2,0},{3,1},{4,2},{5,3},{6,4},{7,5},{8,6},{9,7},{10,8},{11,9},{12,... | collective-permute-start | bytes 589832 | tf_op jit(solution)/shard_map/ppermute | solution.py:22
  17.4 140.3 %collective-permute-start = (bf16[256,384]{0,1:T(8,128)(2,1)S(1)}, bf16[256,384]{0,1:T(8,128)(2,1)}, u32[]{:S(2)}, u32[]{:S(2)}) collective-permute-start(bf16[256,384]{0,1:T(8,128)(2,1)S(1)} %convert_element_type.180), channel_id=1, source_target_pairs={{1,0},{2,1},{3,2},{4,3},{5,4},{6,5},{7,6},{8,7},{9,8},{10,9},{11,1... | collective-permute-start | bytes 589832 | tf_op jit(solution)/shard_map/ppermute | solution.py:22
  31.8 63.2 %collective-permute-start.9 = (bf16[256,384]{0,1:T(8,128)(2,1)}, bf16[256,384]{0,1:T(8,128)(2,1)}, u32[]{:S(2)}, u32[]{:S(2)}) collective-permute-start(bf16[256,384]{0,1:T(8,128)(2,1)} %convert_element_type.189), channel_id=1, source_target_pairs={{2,0},{3,1},{4,2},{5,3},{6,4},{7,5},{8,6},{9,7},{10,8},{11,9},{12,... | collective-permute-start | bytes 589832 | tf_op jit(solution)/shard_map/ppermute | solution.py:22
  76.8 22.0 %collective-permute-start.15 = (bf16[256,384]{0,1:T(8,128)(2,1)}, bf16[256,384]{0,1:T(8,128)(2,1)}, u32[]{:S(2)}, u32[]{:S(2)}) collective-permute-start(bf16[256,384]{0,1:T(8,128)(2,1)} %convert_element_type.189), channel_id=1, source_target_pairs={{3,0},{4,1},{5,2},{6,3},{7,4},{8,5},{9,6},{10,7},{11,8},{12,9},{13... | collective-permute-start | bytes 589832 | tf_op jit(solution)/shard_map/ppermute | solution.py:22
  80.4 28.6 %collective-permute-start.3 = (bf16[256,384]{0,1:T(8,128)(2,1)}, bf16[256,384]{0,1:T(8,128)(2,1)S(1)}, u32[]{:S(2)}, u32[]{:S(2)}) collective-permute-start(bf16[256,384]{0,1:T(8,128)(2,1)} %convert_element_type.189), channel_id=1, source_target_pairs={{1,0},{2,1},{3,2},{4,3},{5,4},{6,5},{7,6},{8,7},{9,8},{10,9},{11,1... | collective-permute-start | bytes 589832 | tf_op jit(solution)/shard_map/ppermute | solution.py:22
  91.8 26.2 %collective-permute-start.21 = (bf16[256,384]{0,1:T(8,128)(2,1)}, bf16[256,384]{0,1:T(8,128)(2,1)S(1)}, u32[]{:S(2)}, u32[]{:S(2)}) collective-permute-start(bf16[256,384]{0,1:T(8,128)(2,1)} %convert_element_type.189), channel_id=1, source_target_pairs={{4,0},{5,1},{6,2},{7,3},{8,4},{9,5},{10,6},{11,7},{12,8},{13,9},{1... | collective-permute-start | bytes 589832 | tf_op jit(solution)/shard_map/ppermute | solution.py:22
  95.0 34.6 %collective-permute-start.7 = (bf16[256,384]{1,0:T(8,128)(2,1)}, bf16[256,384]{1,0:T(8,128)(2,1)S(1)}, u32[]{:S(2)}, u32[]{:S(2)}) collective-permute-start(bf16[256,384]{1,0:T(8,128)(2,1)} %param.8), channel_id=1, source_target_pairs={{2,0},{3,1},{4,2},{5,3},{6,4},{7,5},{8,6},{9,7},{10,8},{11,9},{12,... | collective-permute-start | bytes 589832 | tf_op jit(solution)/shard_map/ppermute | solution.py:22
  98.8 39.6 %collective-permute-start.13 = (bf16[256,384]{1,0:T(8,128)(2,1)}, bf16[256,384]{1,0:T(8,128)(2,1)}, u32[]{:S(2)}, u32[]{:S(2)}) collective-permute-start(bf16[256,384]{1,0:T(8,128)(2,1)} %param.8), channel_id=1, source_target_pairs={{3,0},{4,1},{5,2},{6,3},{7,4},{8,5},{9,6},{10,7},{11,8},{12,9},{13... | collective-permute-start | bytes 589832 | tf_op jit(solution)/shard_map/ppermute | solution.py:22
  109.0 33.1 %collective-permute-start.19 = (bf16[256,384]{1,0:T(8,128)(2,1)}, bf16[256,384]{1,0:T(8,128)(2,1)S(1)}, u32[]{:S(2)}, u32[]{:S(2)}) collective-permute-start(bf16[256,384]{1,0:T(8,128)(2,1)} %param.8), channel_id=1, source_target_pairs={{4,0},{5,1},{6,2},{7,3},{8,4},{9,5},{10,6},{11,7},{12,8},{13,9},{1... | collective-permute-start | bytes 589832 | tf_op jit(solution)/shard_map/ppermute | solution.py:22
  118.0 32.1 %collective-permute-start.1 = (bf16[256,384]{1,0:T(8,128)(2,1)}, bf16[256,384]{1,0:T(8,128)(2,1)}, u32[]{:S(2)}, u32[]{:S(2)}) collective-permute-start(bf16[256,384]{1,0:T(8,128)(2,1)} %param.8), channel_id=1, source_target_pairs={{1,0},{2,1},{3,2},{4,3},{5,4},{6,5},{7,6},{8,7},{9,8},{10,9},{11,1... | collective-permute-start | bytes 589832 | tf_op jit(solution)/shard_map/ppermute | solution.py:22
  130.3 33.9 %collective-permute-start.18 = (bf16[256,384]{0,1:T(8,128)(2,1)S(1)}, bf16[256,384]{0,1:T(8,128)(2,1)S(1)}, u32[]{:S(2)}, u32[]{:S(2)}) collective-permute-start(bf16[256,384]{0,1:T(8,128)(2,1)S(1)} %convert_element_type.180), channel_id=1, source_target_pairs={{4,0},{5,1},{6,2},{7,3},{8,4},{9,5},{10,6},{11,7},{12,8},{13,9},{1... | collective-permute-start | bytes 589832 | tf_op jit(solution)/shard_map/ppermute | solution.py:22
  138.5 654.5 %collective-permute-start.10 = (f32[256,3]{0,1:T(4,128)}, f32[256,3]{0,1:T(4,128)}, u32[]{:S(2)}, u32[]{:S(2)}) collective-permute-start(f32[256,3]{0,1:T(4,128)} %get-tuple-element.59), channel_id=1, source_target_pairs={{0,2},{1,3},{2,4},{3,5},{4,6},{5,7},{6,8},{7,9},{8,10},{9,11},{10,... | collective-permute-start | bytes 9224 | tf_op jit(solution)/shard_map/ppermute | solution.py:22
  142.1 654.2 %collective-permute-start.16 = (f32[256,3]{0,1:T(4,128)}, f32[256,3]{0,1:T(4,128)}, u32[]{:S(2)}, u32[]{:S(2)}) collective-permute-start(f32[256,3]{0,1:T(4,128)} %get-tuple-element.55), channel_id=1, source_target_pairs={{0,3},{1,4},{2,5},{3,6},{4,7},{5,8},{6,9},{7,10},{8,11},{9,12},{10... | collective-permute-start | bytes 9224 | tf_op jit(solution)/shard_map/ppermute | solution.py:22
  150.1 655.3 %collective-permute-start.4 = (f32[256,3]{0,1:T(4,128)}, f32[256,3]{0,1:T(4,128)}, u32[]{:S(2)}, u32[]{:S(2)}) collective-permute-start(f32[256,3]{0,1:T(4,128)} %get-tuple-element.63), channel_id=1, source_target_pairs={{0,1},{1,2},{2,3},{3,4},{4,5},{5,6},{6,7},{7,8},{8,9},{9,10},{10,1... | collective-permute-start | bytes 9224 | tf_op jit(solution)/shard_map/ppermute | solution.py:22
  157.7 674.1 %collective-permute-start.22 = (f32[256,3]{0,1:T(4,128)}, f32[256,3]{0,1:T(4,128)}, u32[]{:S(2)}, u32[]{:S(2)}) collective-permute-start(f32[256,3]{0,1:T(4,128)} %get-tuple-element.53), channel_id=1, source_target_pairs={{0,4},{1,5},{2,6},{3,7},{4,8},{5,9},{6,10},{7,11},{8,12},{9,13},{1... | collective-permute-start | bytes 9224 | tf_op jit(solution)/shard_map/ppermute | solution.py:22
  164.2 648.0 %collective-permute-start.24 = (f32[256,3]{0,1:T(4,128)}, f32[256,3]{0,1:T(4,128)}, u32[]{:S(2)}, u32[]{:S(2)}) collective-permute-start(f32[256,3]{0,1:T(4,128)} %fusion.39), channel_id=1, source_target_pairs={{0,1},{1,2},{2,3},{3,4},{4,5},{5,6},{6,7},{7,8},{8,9},{9,10},{10,1... | collective-permute-start | bytes 9224 | tf_op jit(solution)/shard_map/ppermute | solution.py:22
  793.0 21.7 %collective-permute-start.25 = (f32[256,3]{0,1:T(4,128)}, f32[256,3]{0,1:T(4,128)}, u32[]{:S(2)}, u32[]{:S(2)}) collective-permute-start(f32[256,3]{0,1:T(4,128)} %fusion.43), channel_id=1, source_target_pairs={{0,2},{1,3},{2,4},{3,5},{4,6},{5,7},{6,8},{7,9},{8,10},{9,11},{10,... | collective-permute-start | bytes 9224 | tf_op jit(solution)/shard_map/ppermute | solution.py:22
  796.4 23.3 %collective-permute-start.26 = (f32[256,3]{0,1:T(4,128)}, f32[256,3]{0,1:T(4,128)}, u32[]{:S(2)}, u32[]{:S(2)}) collective-permute-start(f32[256,3]{0,1:T(4,128)} %fusion.47), channel_id=1, source_target_pairs={{0,3},{1,4},{2,5},{3,6},{4,7},{5,8},{6,9},{7,10},{8,11},{9,12},{10... | collective-permute-start | bytes 9224 | tf_op jit(solution)/shard_map/ppermute | solution.py:22
  812.2 26.1 %collective-permute-start.11 = (f32[256,3,128]{0,2,1:T(8,128)}, f32[256,3,128]{0,2,1:T(8,128)S(1)}, u32[]{:S(2)}, u32[]{:S(2)}) collective-permute-start(f32[256,3,128]{0,2,1:T(8,128)} %convolution_bitcast_fusion.14), channel_id=1, source_target_pairs={{0,2},{1,3},{2,4},{3,5},{4,6},{5,7},{6,8},{7,9},{8,10},{9,11},{10,... | collective-permute-start | bytes 1179656 | tf_op jit(solution)/shard_map/ppermute | solution.py:22
  814.7 26.7 %collective-permute-start.17 = (f32[256,3,128]{0,2,1:T(8,128)}, f32[256,3,128]{0,2,1:T(8,128)S(1)}, u32[]{:S(2)}, u32[]{:S(2)}) collective-permute-start(f32[256,3,128]{0,2,1:T(8,128)} %convolution_bitcast_fusion.12), channel_id=1, source_target_pairs={{0,3},{1,4},{2,5},{3,6},{4,7},{5,8},{6,9},{7,10},{8,11},{9,12},{10... | collective-permute-start | bytes 1179656 | tf_op jit(solution)/shard_map/ppermute | solution.py:22
  819.7 33.4 %collective-permute-start.5 = (f32[256,3,128]{0,2,1:T(8,128)}, f32[256,3,128]{0,2,1:T(8,128)S(1)}, u32[]{:S(2)}, u32[]{:S(2)}) collective-permute-start(f32[256,3,128]{0,2,1:T(8,128)} %convolution_bitcast_fusion.16), channel_id=1, source_target_pairs={{0,1},{1,2},{2,3},{3,4},{4,5},{5,6},{6,7},{7,8},{8,9},{9,10},{10,1... | collective-permute-start | bytes 1179656 | tf_op jit(solution)/shard_map/ppermute | solution.py:22
  826.3 42.7 %collective-permute-start.23 = (f32[256,3,128]{0,2,1:T(8,128)}, f32[256,3,128]{0,2,1:T(8,128)S(1)}, u32[]{:S(2)}, u32[]{:S(2)}) collective-permute-start(f32[256,3,128]{0,2,1:T(8,128)} %convolution_bitcast_fusion.10), channel_id=1, source_target_pairs={{0,4},{1,5},{2,6},{3,7},{4,8},{5,9},{6,10},{7,11},{8,12},{9,13},{1... | collective-permute-start | bytes 1179656 | tf_op jit(solution)/shard_map/ppermute | solution.py:22
  (23 other events, 338.1 us)
Sparse Core Ops, SparseCore 0:
  13.3 756.5 all-gather.2
